TPU v7x, 32 devices: a whole 2x2x4 slice. The times are simulated.
32 devices in a mesh: groups: 2 (over y), shard: 16 (over z, x, core).
Axes of the slice: x: 2, y: 2, z: 4, core: 2. Of those that a mesh axis runs over, the one named last changes fastest.
Arguments:
- tokens: bfloat16 [4096, 8192], P(('groups', 'shard')), parts along dimension 0, may hold values from -6 to 6
- base_weight: bfloat16 [8192, 1024], P('shard'), may hold values from -0.0625 to 0.0625
- adapter_ids: int32 [4096, 1], P(('groups', 'shard')), parts along dimension 0, may hold values from 0 to 7; in each aligned block of 128 rows (0 to 127, 128 to 255, ...) at most 17 rows name the same one
- adapter_ranks: int32 [16], P('groups'), parts along dimension 0, may hold values from 16 to 128, as said below
- adapter_owner: int32 [16], P('groups'), parts along dimension 0, may hold values from 0 to 15, as said below
- adapter_down: bfloat16 [32, 8192, 128], P(('groups', 'shard')), parts along dimension 0, may hold values from -0.0625 to 0.0625
- adapter_up: bfloat16 [32, 128, 1024], P(('groups', 'shard')), parts along dimension 0, may hold values from -0.5 to 0.5
- grad_output: bfloat16 [4096, 1024], P(('groups', 'shard')), parts along dimension 0, may hold values from -0.5 to 0.5
Outputs:
- projected: bfloat16 [4096, 1024], P(('groups', 'shard')), parts along dimension 0
- grad_down: float32 [32, 8192, 128], P(('groups', 'shard')), parts along dimension 0
- grad_up: float32 [32, 128, 1024], P(('groups', 'shard')), parts along dimension 0
There are 2 independent parts, one for each index of `groups`. A program takes and returns all parts, laid end to end along the dimension named above; an argument that names none is the same for every part. Nothing has to cross between parts.
Inputs may be any that keep to these rules, and one draw needn't show every extreme that they name: `adapter_ids`: the 128 tokens of one device name one adapter at most 17 times, and some adapter is named that often. `adapter_ranks`: each rank is a multiple of 16; both 16 and 128 occur. `adapter_owner`: adapters are held by distinct devices; devices 0 and 15 hold one each.
All inputs are finite; a program needn't handle non-finite values.
Results may differ from a plain program's by a relative error of at most 0.0034.
Values may be sent and summed in bfloat16 or wider, within the bound.
A program may use at most 128 MiB of HBM per device.

v0:
```python
import jax
import jax.numpy as jnp
from jax import lax
from jax.sharding import PartitionSpec as P


def local(
    tokens,
    base_weight,
    adapter_ids,
    adapter_ranks,
    adapter_owner,
    adapter_down,
    adapter_up,
    grad_output,
):
    device_list = lax.axis_size("shard")
    here_index = lax.axis_index("shard")
    tok_rows, width = tokens.shape
    value_head_width = base_weight.shape[1]
    rank_max = adapter_down.shape[2]
    adapters = adapter_owner.shape[0]
    slot_capacity = (tok_rows + adapters - 1) // adapters + 1
    frozen_output = jnp.dot(
        tokens,
        lax.all_gather(base_weight, "shard", axis=0, tiled=True),
        preferred_element_type=jnp.float32,
    )
    ids_flat = adapter_ids[:, 0]
    match = ids_flat[:, None] == jnp.arange(adapters, dtype=jnp.int32)[None, :]
    target = jnp.sum(jnp.where(match, adapter_owner[None, :], 0), axis=1)
    same = ids_flat[:, None] == ids_flat[None, :]
    earlier = jnp.arange(tok_rows)[:, None] > jnp.arange(tok_rows)[None, :]
    position = jnp.sum((same & earlier).astype(jnp.int32), axis=1)
    slot_position = target * slot_capacity + position
    send_tokens = (
        jnp.zeros((device_list * slot_capacity, width), jnp.bfloat16).at[slot_position].set(tokens)
    )
    send_tokens = send_tokens.reshape(device_list, slot_capacity, width)
    send_grads = (
        jnp.zeros((device_list * slot_capacity, value_head_width), jnp.bfloat16)
        .at[slot_position]
        .set(grad_output)
    )
    send_grads = send_grads.reshape(device_list, slot_capacity, value_head_width)
    recv_tokens, recv_grads = (
        lax.all_to_all(send_tokens, "shard", split_axis=0, concat_axis=0, tiled=True),
        lax.all_to_all(send_grads, "shard", split_axis=0, concat_axis=0, tiled=True),
    )
    rank_here = jnp.sum(jnp.where(adapter_owner == here_index, adapter_ranks, 0))
    rank_safe = jnp.where(rank_here > 0, rank_here, 16)
    scale = 32.0 / rank_safe.astype(jnp.float32)
    keep = jnp.arange(rank_max, dtype=jnp.int32) < rank_here
    token_block = recv_tokens.reshape(device_list * slot_capacity, width)
    hidden = jnp.where(
        keep[None, :],
        jnp.dot(token_block, adapter_down[0], preferred_element_type=jnp.float32),
        0.0,
    ).astype(jnp.bfloat16)
    lowrank_update = (
        scale * jnp.dot(hidden, adapter_up[0], preferred_element_type=jnp.float32)
    ).astype(jnp.bfloat16)
    gathered_back = lax.all_to_all(
        lowrank_update.reshape(device_list, slot_capacity, value_head_width),
        "shard",
        split_axis=0,
        concat_axis=0,
        tiled=True,
    )
    lowrank_branch = gathered_back.reshape(device_list * slot_capacity, value_head_width)[
        slot_position
    ]
    projected = (frozen_output + lowrank_branch.astype(jnp.float32)).astype(jnp.bfloat16)
    grad_block = recv_grads.reshape(device_list * slot_capacity, value_head_width)
    back = lax.dot_general(
        grad_block, adapter_up[0], (((1,), (1,)), ((), ())), preferred_element_type=jnp.float32
    )
    low_rank = jnp.where(keep[None, :], scale * back, 0.0).astype(jnp.bfloat16)
    grad_down = lax.dot_general(
        token_block, low_rank, (((0,), (0,)), ((), ())), preferred_element_type=jnp.float32
    )
    grad_up = scale * lax.dot_general(
        hidden, grad_block, (((0,), (0,)), ((), ())), preferred_element_type=jnp.float32
    )
    return (projected, grad_down[None], grad_up[None])


def solution(mesh):
    in_specs = (
        P(("groups", "shard"), None),
        P("shard", None),
        P(("groups", "shard"), None),
        P("groups"),
        P("groups"),
        P(("groups", "shard"), None, None),
        P(("groups", "shard"), None, None),
        P(("groups", "shard"), None),
    )
    out_specs = (
        P(("groups", "shard"), None),
        P(("groups", "shard"), None, None),
        P(("groups", "shard"), None, None),
    )
    return jax.shard_map(local, mesh=mesh, in_specs=in_specs, out_specs=out_specs, check_vma=False)
```

profile of v0, /device:TPU:1, one launch (start us, length us, event | category | flops | bytes accessed | tf_op | source)
XLA Modules:
  0.0 326.3 jit_solution(3047518683033937409)
XLA Ops:
  7.2 0.0 copy-start
  7.2 0.0 all-gather.2.cloned.1.call-start
  7.2 0.7 all-gather.2.cloned.1.call-update
  7.9 0.8 select_reduce_fusion
  8.7 0.9 convert_reduce_fusion
  9.6 7.1 %scatter_custom_fusion = bf16[272,8192]{1,0:T(8,128)(2,1)} fusion(s32[128]{0:T(128)S(1)} %fusion.25, bf16[128,8192]{1,0:T(8,128)(2,1)} %param.8, bf16[]{:T(256)} %constant.2.clone.1), kind=kCustom, calls=%fused_computation.4 | custom fusion | bytes 4456960 | tf_op jit(solution)/shard_map/scatter | solution.py:37
  16.7 5.3 %reshape.56 = bf16[16,17,8192]{2,1,0:T(8,128)(2,1)} reshape(bf16[272,8192]{1,0:T(8,128)(2,1)} %scatter_custom_fusion) | data formatting | bytes 8912896 | tf_op jit(solution)/shard_map/reshape | solution.py:39
  22.1 0.0 copy-start.2
  22.1 0.0 copy-start.3
  22.1 7.4 %all-to-all-start = ((bf16[16,17,8192]{2,1,0:T(8,128)(2,1)}), bf16[16,17,8192]{2,1,0:T(8,128)(2,1)}, u32[]{:S(2)}, u32[]{:S(2)}) async-start(bf16[16,17,8192]{2,1,0:T(8,128)(2,1)} %reshape.56), calls=%async_computation | async-start | bytes 12582912 | tf_op jit(solution)/shard_map/all_to_all | solution.py:47
  29.4 1.7 scatter_custom_fusion.1
  31.2 1.1 reshape.60
  32.2 195.7 %all-to-all-done = bf16[16,17,8192]{2,1,0:T(8,128)(2,1)} async-done(((bf16[16,17,8192]{2,1,0:T(8,128)(2,1)}), bf16[16,17,8192]{2,1,0:T(8,128)(2,1)}, u32[]{:S(2)}, u32[]{:S(2)}) %all-to-all-start) | async-done | bytes 4456480 | tf_op jit(solution)/shard_map/all_to_all | solution.py:47
  228.0 36.9 %all-to-all-start.2 = ((bf16[16,17,1024]{2,1,0:T(8,128)(2,1)}), bf16[16,17,1024]{2,1,0:T(8,128)(2,1)S(1)}, u32[]{:S(2)}, u32[]{:S(2)}) async-start(bf16[16,17,1024]{2,1,0:T(8,128)(2,1)} %reshape.60), calls=%async_computation.2 | async-start | bytes 1572864 | tf_op jit(solution)/shard_map/all_to_all | solution.py:48
  264.9 0.0 copy-done.2
  264.9 0.0 copy-done.3
  264.9 0.6 fusion.24
  266.9 0.7 iota_compare_fusion.2
  267.5 5.2 %reshape.57 = bf16[272,8192]{1,0:T(8,128)(2,1)} reshape(bf16[16,17,8192]{2,1,0:T(8,128)(2,1)} %all-to-all-done) | data formatting | bytes 8912896 | tf_op jit(solution)/shard_map/reshape | solution.py:54
  272.7 0.0 copy-done
  272.7 0.0 copy-start.1
  272.7 3.6 %fusion.11 = bf16[272,128]{1,0:T(8,128)(2,1)S(1)} fusion(bf16[272,8192]{1,0:T(8,128)(2,1)} %reshape.57, bf16[1,8192,128]{2,1,0:T(8,128)(2,1)S(1)} %copy-done, pred[128]{0:T(512)(128)(4,1)S(1)} %iota_compare_fusion.2), kind=kOutput, calls=%fused_computation.17 | convolution fusion | flops 570494976 | bytes 6623360 | tf_op jit(solution)/shard_map/dot_general | solution.py:57
  276.3 0.0 copy-done.1
  276.4 0.3 fusion.4
  276.7 1.1 reshape.58
  277.8 5.7 %all-to-all-done.2 = bf16[16,17,1024]{2,1,0:T(8,128)(2,1)S(1)} async-done(((bf16[16,17,1024]{2,1,0:T(8,128)(2,1)}), bf16[16,17,1024]{2,1,0:T(8,128)(2,1)S(1)}, u32[]{:S(2)}, u32[]{:S(2)}) %all-to-all-start.2) | async-done | bytes 557088 | tf_op jit(solution)/shard_map/all_to_all | solution.py:48
  283.4 5.6 %all-to-all-start.1 = ((bf16[16,17,1024]{2,1,0:T(8,128)(2,1)}), bf16[16,17,1024]{2,1,0:T(8,128)(2,1)}, u32[]{:S(2)}, u32[]{:S(2)}) async-start(bf16[16,17,1024]{2,1,0:T(8,128)(2,1)} %reshape.58), calls=%async_computation.1 | async-start | bytes 1572864 | tf_op jit(solution)/shard_map/all_to_all | solution.py:63
  289.1 0.2 reshape.61
  289.3 1.1 fusion.5
  290.4 6.7 %convolution_bitcast_fusion = f32[1,8192,128]{2,1,0:T(8,128)} fusion(bf16[272,8192]{1,0:T(8,128)(2,1)} %reshape.57, bf16[272,1024]{1,0:T(8,128)(2,1)S(1)} %reshape.61, bf16[1,128,1024]{2,1,0:T(8,128)(2,1)} %param.14, f32[]{:T(128)S(6)} %div.3, pred[128]{0:T(512)(128)(4,1)S(1)} %iota_compare_fusion.2), kind=kOutput, calls=%fused_computation.3 | convolution fusion | flops 641832960 | bytes 9470084 | tf_op jit(solution)/shard_map/dot_general | solution.py:79
  297.1 10.6 %all-to-all-done.1 = bf16[16,17,1024]{2,1,0:T(8,128)(2,1)} async-done(((bf16[16,17,1024]{2,1,0:T(8,128)(2,1)}), bf16[16,17,1024]{2,1,0:T(8,128)(2,1)}, u32[]{:S(2)}, u32[]{:S(2)}) %all-to-all-start.1) | async-done | bytes 557088 | tf_op jit(solution)/shard_map/all_to_all | solution.py:63
  307.7 1.3 reshape.59
  309.1 0.9 gather_fusion
  309.9 0.0 all-gather.2.cloned.1.call-done
  310.0 9.5 %fusion.6 = bf16[128,1024]{1,0:T(8,128)(2,1)} fusion(bf16[128,8192]{1,0:T(8,128)(2,1)} %param.8, bf16[8192,1024]{1,0:T(8,128)(2,1)} %all-gather.2.cloned.1.call-done, bf16[128,1024]{1,0:T(8,128)(2,1)S(1)} %gather_fusion), kind=kOutput, calls=%fused_computation.13 | convolution fusion | flops 2147876864 | bytes 19398656 | tf_op jit(solution)/shard_map/dot_general | solution.py:24
  (2 shorter events, 0.0 us)
Async XLA Ops:
  7.2 265.6 %copy-start = (bf16[1,8192,128]{2,1,0:T(8,128)(2,1)S(1)}, bf16[1,8192,128]{2,1,0:T(8,128)(2,1)}, u32[]{:S(2)}) copy-start(bf16[1,8192,128]{2,1,0:T(8,128)(2,1)} %param.13) | copy-start | bytes 6291460
  7.2 302.8 %all-gather.2.cloned.1.call-start = ((), (), s32[]{:S(2)}) async-start(), calls=%async_computation.3 | async-start | bytes 17825792 | tf_op jit(solution)/shard_map/all_gather | solution.py:26
  22.1 242.8 %copy-start.2 = (s32[8]{0:T(128)S(1)}, s32[8]{0:T(128)}, u32[]{:S(2)}) copy-start(s32[8]{0:T(128)} %param.12) | copy-start | bytes 100
  22.1 242.8 %copy-start.3 = (s32[8]{0:T(128)S(1)}, s32[8]{0:T(128)}, u32[]{:S(2)}) copy-start(s32[8]{0:T(128)} %param.11) | copy-start | bytes 100
  22.1 205.9 %all-to-all-start = ((bf16[16,17,8192]{2,1,0:T(8,128)(2,1)}), bf16[16,17,8192]{2,1,0:T(8,128)(2,1)}, u32[]{:S(2)}, u32[]{:S(2)}) async-start(bf16[16,17,8192]{2,1,0:T(8,128)(2,1)} %reshape.56), calls=%async_computation | async-start | bytes 12582912 | tf_op jit(solution)/shard_map/all_to_all | solution.py:47
  228.0 55.5 %all-to-all-start.2 = ((bf16[16,17,1024]{2,1,0:T(8,128)(2,1)}), bf16[16,17,1024]{2,1,0:T(8,128)(2,1)S(1)}, u32[]{:S(2)}, u32[]{:S(2)}) async-start(bf16[16,17,1024]{2,1,0:T(8,128)(2,1)} %reshape.60), calls=%async_computation.2 | async-start | bytes 1572864 | tf_op jit(solution)/shard_map/all_to_all | solution.py:48
  272.7 3.6 %copy-start.1 = (bf16[1,128,1024]{2,1,0:T(8,128)(2,1)S(1)}, bf16[1,128,1024]{2,1,0:T(8,128)(2,1)}, u32[]{:S(2)}) copy-start(bf16[1,128,1024]{2,1,0:T(8,128)(2,1)} %param.14) | copy-start | bytes 786436
  283.4 24.3 %all-to-all-start.1 = ((bf16[16,17,1024]{2,1,0:T(8,128)(2,1)}), bf16[16,17,1024]{2,1,0:T(8,128)(2,1)}, u32[]{:S(2)}, u32[]{:S(2)}) async-start(bf16[16,17,1024]{2,1,0:T(8,128)(2,1)} %reshape.58), calls=%async_computation.1 | async-start | bytes 1572864 | tf_op jit(solution)/shard_map/all_to_all | solution.py:63
Sparse Core Ops, SparseCore 0:
  10.2 237.6 all-gather.1
where the time goes:
time: 327 us; the launch traced here: 326 us
  waiting for transfers between devices  213 us (65%)
  starting transfers between devices  50 us (15%)
  local copies, waits for them, and re-layouts  24 us (7%)
  matrix products  21.2 us (6%)
  between operations  15.5 us (5%)
    all_to_all x1, waiting for transfers between devices, local(): lax.all_to_all(send_tokens, 'shard', split_axis=0, concat_axis=0, tiled=T...  196 us
    all_to_all x1, starting transfers between devices, local(): lax.all_to_all(send_grads, 'shard', split_axis=0, concat_axis=0, tiled=True)  36.9 us
    all_to_all x1, waiting for transfers between devices, local(): lax.all_to_all(lowrank_update.reshape(device_list, slot_capacity, value_h...  10.6 us
    dot_general x1, matrix products, local(): jnp.dot(tokens, lax.all_gather(base_weight, 'shard', axis=0, tiled=True),...  9.45 us
    all_to_all x1, starting transfers between devices, local(): lax.all_to_all(send_tokens, 'shard', split_axis=0, concat_axis=0, tiled=T...  7.35 us
    scatter x1, local copies, waits for them, and re-layouts, local(): jnp.zeros((device_list * slot_capacity, width), jnp.bfloat16)  7.15 us
    dot_general x1, matrix products, local(): lax.dot_general(token_block, low_rank, (((0,), (0,)), ((), ())), preferre...  6.67 us
  transfers between devices with their start and end apart: 4, of which 3 were waited for; matrix products, arithmetic and copies ran while one was open for 12% of the time, Pallas kernels for 0%

commit v1 on v0

v1 whole, which is shorter than its diff:
```python
import functools

import jax
import jax.numpy as jnp
from jax import lax
from jax.experimental import pallas as pl
from jax.experimental.pallas import tpu as pltpu
from jax.sharding import PartitionSpec as P

MESH = pl.DeviceIdType.MESH
QUAD = 4


def remote(src, dst, send, recv, to):
    return pltpu.make_async_remote_copy(
        src_ref=src, dst_ref=dst, send_sem=send, recv_sem=recv,
        device_id={"shard": to}, device_id_type=MESH,
    )


def greet_all(n, me):
    barrier = pltpu.get_barrier_semaphore()

    @pl.loop(1, n)
    def _(k):
        pl.semaphore_signal(
            barrier, inc=1, device_id={"shard": lax.rem(me + k, n)}, device_id_type=MESH
        )

    pl.semaphore_wait(barrier, n - 1)


def exchange_copy(n, me, k, src, dst, send, recv):
    to = lax.rem(me + k, n)
    return remote(src.at[to], dst.at[me], send.at[k], recv.at[k], to)


def start_exchange(n, me, pairs, send, recv, own):
    for i, (src, dst) in enumerate(pairs):
        pltpu.make_async_copy(src.at[me], dst.at[me], own.at[i]).start()

    @pl.loop(1, n)
    def _(k):
        for i, (src, dst) in enumerate(pairs):
            exchange_copy(n, me, k, src, dst, send.at[i], recv.at[i]).start()


def finish_exchange(n, me, pairs, send, recv, own):
    for i, (src, dst) in enumerate(pairs):
        pltpu.make_async_copy(src.at[me], dst.at[me], own.at[i]).wait()

    @pl.loop(1, n)
    def _(k):
        for i, (src, dst) in enumerate(pairs):
            exchange_copy(n, me, k, src, dst, send.at[i], recv.at[i]).wait()


def back_kernel(n, count, *refs):
    pairs = list(zip(refs[:count], refs[count:2 * count]))
    send, recv, own = refs[2 * count:]
    me = lax.axis_index("shard")
    greet_all(n, me)
    start_exchange(n, me, pairs, send, recv, own)
    finish_exchange(n, me, pairs, send, recv, own)


def forward_kernel(n, count, *refs):
    ins, outs = refs[:count], refs[count + 2:2 * count + 2]
    quarters_ref, weight_ref = refs[count:count + 2]
    base_ref = refs[2 * count + 2]
    (quad_tokens, weights, partial, partial_in, send, recv, own,
     w_right, w_left, w_recv, t_send, t_recv, p_send, p_recv, local_sem) = refs[2 * count + 3:]
    pairs = list(zip(ins, outs))
    me = lax.axis_index("shard")
    lines = n // QUAD
    row, col = me // QUAD, lax.rem(me, QUAD)
    depth = weight_ref.shape[0]

    def block(j):
        return weights.at[pl.ds(pl.multiple_of(j * depth, depth), depth)]

    def to_right(j):
        return remote(block(j), block(j), w_right.at[j], w_recv.at[j], me + QUAD)

    def to_left(j):
        return remote(block(j), block(j), w_left.at[j], w_recv.at[j], me - QUAD)

    def token_copy(k):
        other = lax.rem(col + k, QUAD)
        return remote(quarters_ref.at[other], quad_tokens.at[col], t_send.at[k], t_recv.at[k],
                      row * QUAD + other)

    def partial_copy(k):
        other = lax.rem(col + k, QUAD)
        return remote(partial.at[other], partial_in.at[col], p_send.at[k], p_recv.at[k],
                      row * QUAD + other)

    own_weight = pltpu.make_async_copy(weight_ref, block(row), local_sem.at[0])
    own_tokens = pltpu.make_async_copy(quarters_ref.at[col], quad_tokens.at[col], local_sem.at[1])
    own_weight.start()
    own_tokens.start()
    greet_all(n, me)
    own_weight.wait()

    @pl.when(row < lines - 1)
    def _():
        to_right(row).start()

    @pl.when(row > 0)
    def _():
        to_left(row).start()

    for k in range(1, QUAD):
        token_copy(k).start()
    start_exchange(n, me, pairs, send, recv, own)

    @pl.loop(1, lines)
    def _(t):
        @pl.when(row - t >= 0)
        def _():
            to_right(row - t).wait_recv()

            @pl.when(row < lines - 1)
            def _():
                to_right(row - t).start()

        @pl.when(row + t <= lines - 1)
        def _():
            to_left(row + t).wait_recv()

            @pl.when(row > 0)
            def _():
                to_left(row + t).start()

    own_tokens.wait()
    for k in range(1, QUAD):
        token_copy(k).wait()
    for k in (1, 2, 3, 0):
        other = lax.rem(col + k, QUAD)
        partial[other] = jnp.dot(
            quad_tokens[other], weights[...], preferred_element_type=jnp.float32
        )
        if k > 0:
            partial_copy(k).start()
    total = partial[col]
    for k in range(1, QUAD):
        partial_copy(k).wait()
        total = total + partial_in[lax.rem(col - k + QUAD, QUAD)]
    base_ref[...] = total

    @pl.when(row < lines - 1)
    def _():
        @pl.loop(0, row + 1)
        def _(j):
            to_right(j).wait_send()

    @pl.when(row > 0)
    def _():
        @pl.loop(row, lines)
        def _(j):
            to_left(j).wait_send()

    finish_exchange(n, me, pairs, send, recv, own)


def exchange_sems(n, count):
    return [pltpu.SemaphoreType.DMA((count, n)), pltpu.SemaphoreType.DMA((count, n)),
            pltpu.SemaphoreType.DMA((count,))]


ANY = pl.BlockSpec(memory_space=pl.ANY)
VMEM = pl.BlockSpec(memory_space=pltpu.VMEM)


def forward(n, sends, quarters, base_weight):
    count = len(sends)
    lines = n // QUAD
    rows, quarter = quarters.shape[1:]
    wide = base_weight.shape[1]
    dma = pltpu.SemaphoreType.DMA
    return pl.pallas_call(
        functools.partial(forward_kernel, n, count),
        out_shape=[jax.ShapeDtypeStruct(s.shape, s.dtype) for s in sends]
        + [jax.ShapeDtypeStruct((rows, wide), jnp.float32)],
        in_specs=[ANY] * (count + 2),
        out_specs=[ANY] * count + [VMEM],
        scratch_shapes=[
            pltpu.VMEM((QUAD, rows, quarter), jnp.bfloat16),
            pltpu.VMEM((quarter, wide), jnp.bfloat16),
            pltpu.VMEM((QUAD, rows, wide), jnp.float32),
            pltpu.VMEM((QUAD, rows, wide), jnp.float32),
        ] + exchange_sems(n, count) + [dma((lines,))] * 3 + [dma((QUAD,))] * 4 + [dma((2,))],
        compiler_params=pltpu.CompilerParams(
            collective_id=0, has_side_effects=True, vmem_limit_bytes=40 * 2**20
        ),
    )(*sends, quarters, base_weight)


def back(n, sends):
    count = len(sends)
    return pl.pallas_call(
        functools.partial(back_kernel, n, count),
        out_shape=[jax.ShapeDtypeStruct(s.shape, s.dtype) for s in sends],
        in_specs=[ANY] * count,
        out_specs=[ANY] * count,
        scratch_shapes=exchange_sems(n, count),
        compiler_params=pltpu.CompilerParams(collective_id=1, has_side_effects=True),
    )(*sends)


def packed(x):
    n, cells = x.shape
    return jnp.pad(x, ((0, 0), (0, -cells % 2048))).reshape(n, 16, -1)


def unpacked(x, cells):
    return x.reshape(x.shape[0], -1)[:, :cells]


def local(
    tokens,
    base_weight,
    adapter_ids,
    adapter_ranks,
    adapter_owner,
    adapter_down,
    adapter_up,
    grad_output,
):
    n = lax.axis_size("shard")
    here_index = lax.axis_index("shard")
    rows, width = tokens.shape
    wide = base_weight.shape[1]
    rank_max = adapter_down.shape[2]
    adapters = adapter_owner.shape[0]
    capacity = (rows + adapters - 1) // adapters + 1
    whole = capacity // 16 * 16
    rest = capacity - whole
    lines = n // QUAD
    both = width + wide
    bf16, f32 = jnp.bfloat16, jnp.float32

    ids = adapter_ids[:, 0]
    match = ids[:, None] == jnp.arange(adapters, dtype=jnp.int32)[None, :]
    target = jnp.sum(jnp.where(match, adapter_owner[None, :], 0), axis=1)
    same = ids[:, None] == ids[None, :]
    earlier = jnp.arange(rows)[:, None] > jnp.arange(rows)[None, :]
    position = jnp.sum((same & earlier).astype(jnp.int32), axis=1)

    joined = jnp.concatenate([tokens, grad_output], axis=1)
    sends, picks = [], []
    if whole:
        slot = jnp.where(position < whole, target * whole + position, -1)
        pick = (jnp.arange(n * whole)[:, None] == slot[None, :]).astype(bf16)
        picks.append(pick)
        sends.append(
            jnp.dot(pick, joined, preferred_element_type=bf16).reshape(n, whole, both)
        )
    if rest:
        slot = jnp.where(position >= whole, target * rest + position - whole, -1)
        pick = (jnp.arange(n * rest)[:, None] == slot[None, :]).astype(bf16)
        picks.append(pick)
        sends.append(packed(
            jnp.dot(pick, joined, preferred_element_type=bf16).reshape(n, rest * both)
        ))
    quarters = tokens.reshape(rows, lines, QUAD, -1).transpose(2, 0, 1, 3).reshape(QUAD, rows, -1)

    got = forward(n, sends, quarters, base_weight)
    base = got[-1]
    blocks = []
    if whole:
        blocks.append(got[0].reshape(n * whole, both))
    if rest:
        blocks.append(unpacked(got[-2], rest * both).reshape(n * rest, both))

    rank_here = jnp.sum(jnp.where(adapter_owner == here_index, adapter_ranks, 0))
    rank_safe = jnp.where(rank_here > 0, rank_here, 16)
    scale = 32.0 / rank_safe.astype(f32)
    keep = jnp.arange(rank_max, dtype=jnp.int32) < rank_here
    block = jnp.concatenate(blocks, axis=0)
    token_block, grad_block = block[:, :width], block[:, width:]
    hidden = jnp.where(
        keep[None, :],
        jnp.dot(token_block, adapter_down[0], preferred_element_type=f32),
        0.0,
    ).astype(bf16)
    update = (scale * jnp.dot(hidden, adapter_up[0], preferred_element_type=f32)).astype(bf16)
    sends = []
    if whole:
        sends.append(update[:n * whole].reshape(n, whole, wide))
    if rest:
        sends.append(packed(update[n * whole:].reshape(n, rest * wide)))
    got = back(n, sends)
    blocks = []
    if whole:
        blocks.append(got[0].reshape(n * whole, wide))
    if rest:
        blocks.append(unpacked(got[-1], rest * wide).reshape(n * rest, wide))
    branch = sum(
        lax.dot_general(p, b, (((0,), (0,)), ((), ())), preferred_element_type=f32)
        for p, b in zip(picks, blocks)
    )
    projected = (base + branch).astype(bf16)
    grad_low = lax.dot_general(
        grad_block, adapter_up[0], (((1,), (1,)), ((), ())), preferred_element_type=f32
    )
    low = jnp.where(keep[None, :], scale * grad_low, 0.0).astype(bf16)
    grad_down = lax.dot_general(
        token_block, low, (((0,), (0,)), ((), ())), preferred_element_type=f32
    )
    grad_up = scale * lax.dot_general(
        hidden, grad_block, (((0,), (0,)), ((), ())), preferred_element_type=f32
    )
    return (projected, grad_down[None], grad_up[None])


def solution(mesh):
    in_specs = (
        P(("groups", "shard"), None),
        P("shard", None),
        P(("groups", "shard"), None),
        P("groups"),
        P("groups"),
        P(("groups", "shard"), None, None),
        P(("groups", "shard"), None, None),
        P(("groups", "shard"), None),
    )
    out_specs = (
        P(("groups", "shard"), None),
        P(("groups", "shard"), None, None),
        P(("groups", "shard"), None, None),
    )
    return jax.shard_map(local, mesh=mesh, in_specs=in_specs, out_specs=out_specs, check_vma=False)
```

time: 327 us -> 273 us (0.83)
  Pallas kernels: 0 us -> 222 us
  waiting for transfers between devices: 213 us -> 0 us
  starting transfers between devices: 50 us -> 0 us
  between operations: 15.5 us -> 2.23 us
  matrix products: 21.2 us -> 17.7 us
    pallas_call x0 -> x2, Pallas kernels: none -> 222 us  [the longest x1 209 us: forward(): pl.pallas_call(functools.partial(forward_kernel, n, count), out_shape=[ja...]
    all_to_all x3 -> x0, waiting for transfers between devices: 212 us -> none  [the longest x1 196 us: local(): lax.all_to_all(send_tokens, 'shard', split_axis=0, concat_axis=0, tiled=T...]
    all_to_all x3 -> x0, starting transfers between devices: 49.9 us -> none  [the longest x1 36.9 us: local(): lax.all_to_all(send_grads, 'shard', split_axis=0, concat_axis=0, tiled=True)]
    unnamed x8 -> x28, local copies, waits for them, and re-layouts: 0.02 us -> 10.2 us
    scatter x2 -> x0, local copies, waits for them, and re-layouts: 8.88 us -> none  [the longest x1 7.15 us: local(): jnp.zeros((device_list * slot_capacity, width), jnp.bfloat16)]
    dot_general x4 -> x7, matrix products: 20 us -> 16.6 us  [the longest x1 6.57 us: local(): lax.dot_general(token_block, low, (((0,), (0,)), ((), ())), preferred_ele...]
    reshape x6 -> x3, local copies, waits for them, and re-layouts: 14.2 us -> 12.8 us  [local(): tokens.reshape(rows, lines, QUAD, -1).transpose(2, 0, 1, 3)]
  transfers between devices with their start and end apart: 4 -> 0, of which waited for: 3 -> 0; matrix products, arithmetic and copies ran while one was open for 12% -> 0% of each run, Pallas kernels for 0% -> 0%
where the time goes in v1:
time: 273 us; the launch traced here: 270 us
  Pallas kernels  222 us (81%)
  local copies, waits for them, and re-layouts  23.9 us (9%)
  matrix products  17.7 us (6%)
  other arithmetic  4.13 us (2%)
    pallas_call x1, Pallas kernels, forward(): pl.pallas_call(functools.partial(forward_kernel, n, count), out_shape=[ja...  209 us
    pallas_call x1, Pallas kernels, back(): pl.pallas_call(functools.partial(back_kernel, n, count), out_shape=[jax.S...  13.7 us
    reshape x3, local copies, waits for them, and re-layouts, local(): tokens.reshape(rows, lines, QUAD, -1).transpose(2, 0, 1, 3)  12.8 us
    unnamed x28, local copies, waits for them, and re-layouts  10.2 us
    dot_general x1, matrix products, local(): lax.dot_general(token_block, low, (((0,), (0,)), ((), ())), preferred_ele...  6.57 us

profile of v1, /device:TPU:1, one launch (start us, length us, event | category | flops | bytes accessed | tf_op | source)
XLA Modules:
  0.0 270.3 jit_solution(278038006124334401)
XLA Ops:
  0.6 0.0 copy-start
  0.6 0.0 copy-start.8
  0.7 1.0 convert_reduce_fusion
  1.7 0.8 select_reduce_fusion
  2.4 1.7 constant_dynamic-update-slice_fusion.1
  4.2 0.0 copy-done.8
  4.2 3.5 %fusion.19 = bf16[256,9216]{1,0:T(8,128)(2,1)} fusion(bf16[128,9216]{1,0:T(8,128)(2,1)S(1)} %constant_dynamic-update-slice_fusion, s32[128]{0:T(128)S(1)} %get-tuple-element.14), kind=kOutput, calls=%fused_computation.24 | convolution fusion | flops 604012544 | bytes 7078400 | tf_op jit(solution)/shard_map/dot_general | solution.py:257
  7.7 0.4 fusion.27
  8.2 4.5 %reshape.60 = bf16[128,4,4,512]{3,2,1,0:T(4,128)(2,1)} reshape(bf16[128,8192]{1,0:T(8,128)(2,1)} %param.8) | data formatting | bytes 4194304 | tf_op jit(solution)/shard_map/reshape | solution.py:266
  12.7 0.0 copy-start.4
  12.7 3.9 %copy.19 = bf16[128,4,4,512]{3,1,0,2:T(4,128)(2,1)} copy(bf16[128,4,4,512]{3,2,1,0:T(4,128)(2,1)} %reshape.60) | data formatting | bytes 4194304 | tf_op jit(solution)/shard_map/reshape | solution.py:266
  16.6 4.4 %reshape.61.refs_2_ = bf16[4,128,2048]{2,1,0:T(8,128)(2,1)} reshape(bf16[4,128,4,512]{3,2,1,0:T(4,128)(2,1)} %bitcast.49) | data formatting | bytes 4194304 | tf_op jit(solution)/shard_map/reshape | solution.py:266
  21.0 0.0 copy-done.4
  21.0 0.0 copy-start.1
  21.0 2.3 copy-done.1
  23.4 0.0 copy-start.2
  23.4 1.6 copy-done.2
  25.0 0.0 copy-start.9
  25.0 0.0 copy-start.10
  25.0 208.6 %shard_map.103 = (bf16[16,16,9216]{2,1,0:T(8,128)(2,1)S(1)}, bf16[16,16,640]{2,1,0:T(8,128)(2,1)S(1)}, f32[128,1024]{1,0:T(8,128)S(1)}) custom-call(bf16[16,16,9216]{2,1,0:T(8,128)(2,1)S(1)} %bitcast.43, bf16[16,16,640]{2,1,0:T(8,128)(2,1)S(1)} %bitcast.47, bf16[4,128,2048]{2,1,0:T(8,128)(2,1)S(1)} %copy-done.2, bf16[512,1024]{1,0:T(8,128)(2,1)S(1)} %copy-done.4), custom_call_target="tpu_custom_call" | custom-call | tf_op jit(solution)/shard_map/pallas_call | solution.py:181
  233.6 0.0 copy-start.3
  233.6 2.1 copy-done.3
  235.7 0.0 copy-start.5
  235.7 0.8 copy-done.5
  236.5 0.1 copy.14
  236.6 0.0 copy-done.9
  236.6 0.0 copy-done.10
  236.6 0.6 fusion.30
  237.3 0.6 iota_compare_fusion.8
  237.9 0.0 copy-done
  237.9 0.0 copy-start.7
  238.0 3.5 %fusion.11 = bf16[272,128]{1,0:T(8,128)(2,1)S(1)} fusion(bf16[1,8192,128]{2,1,0:T(8,128)(2,1)S(1)} %copy-done, pred[128]{0:T(512)(128)(4,1)S(1)} %iota_compare_fusion.8, bf16[256,9216]{1,0:T(8,128)(2,1)} %bitcast.44, bf16[16,9216]{1,0:T(8,128)(2,1)S(1)} %slice.24), kind=kOutput, calls=%fused_computation.17 | convolution fusion | flops 579407872 | bytes 7180416 | tf_op jit(solution)/shard_map/dot_general | solution.py:284
  241.5 0.0 copy-start.6
  242.9 0.0 copy-done.7
  242.9 0.3 fusion.3
  243.2 0.8 slice.27
  244.1 0.6 copy.15
  244.7 13.7 %shard_map.104 = (bf16[16,16,1024]{2,1,0:T(8,128)(2,1)}, bf16[16,16,128]{2,1,0:T(8,128)(2,1)}) custom-call(bf16[16,16,1024]{2,1,0:T(8,128)(2,1)} %bitcast.50, bf16[16,16,128]{2,1,0:T(8,128)(2,1)} %bitcast.54), custom_call_target="tpu_custom_call" | custom-call | tf_op jit(solution)/shard_map/pallas_call | solution.py:201
  258.4 1.3 fusion.18
  259.7 0.9 copy.20
  260.6 0.0 copy-done.6
  260.6 1.0 fusion.6
  261.6 1.1 pad_maximum_fusion
  262.7 1.1 fusion.5
  263.8 6.6 %convolution_bitcast_fusion = f32[1,8192,128]{2,1,0:T(8,128)} fusion(bf16[272,1024]{1,0:T(8,128)(2,1)S(1)} %pad_maximum_fusion, bf16[1,128,1024]{2,1,0:T(8,128)(2,1)S(1)} %copy-done.7, f32[]{:T(128)S(6)} %div.3, pred[128]{0:T(512)(128)(4,1)S(1)} %iota_compare_fusion.8, bf16[256,9216]{1,0:T(8,128)(2,1)} %bitcast.46, bf16[16,9216]{1,0:T(8,128)(2,1)S(1)} %slice.24), kind=kOutput, calls=%fused_computation | convolution fusion | flops 650745856 | bytes 10027140 | tf_op jit(solution)/shard_map/dot_general | solution.py:308
  (7 shorter events, 0.1 us)
Async XLA Ops:
  0.6 237.3 %copy-start = (bf16[1,8192,128]{2,1,0:T(8,128)(2,1)S(1)}, bf16[1,8192,128]{2,1,0:T(8,128)(2,1)}, u32[]{:S(2)}) copy-start(bf16[1,8192,128]{2,1,0:T(8,128)(2,1)} %param.13) | copy-start | bytes 6291460
  0.6 3.5 %copy-start.8 = (bf16[128,1024]{1,0:T(8,128)(2,1)S(1)}, bf16[128,1024]{1,0:T(8,128)(2,1)}, u32[]{:S(2)}) copy-start(bf16[128,1024]{1,0:T(8,128)(2,1)} %param.15) | copy-start | bytes 786436
  12.7 8.3 %copy-start.4 = (bf16[512,1024]{1,0:T(8,128)(2,1)S(1)}, bf16[512,1024]{1,0:T(8,128)(2,1)}, u32[]{:S(2)}) copy-start(bf16[512,1024]{1,0:T(8,128)(2,1)} %refs_3_.1) | copy-start | bytes 3145732
  21.0 2.3 copy-start.1
  23.4 1.6 copy-start.2
  25.0 211.7 %copy-start.9 = (s32[8]{0:T(128)S(1)}, s32[8]{0:T(128)}, u32[]{:S(2)}) copy-start(s32[8]{0:T(128)} %param.12) | copy-start | bytes 100
  25.0 211.7 %copy-start.10 = (s32[8]{0:T(128)S(1)}, s32[8]{0:T(128)}, u32[]{:S(2)}) copy-start(s32[8]{0:T(128)} %param.11) | copy-start | bytes 100
  233.6 2.1 copy-start.3
  235.7 0.8 copy-start.5
  237.9 5.0 %copy-start.7 = (bf16[1,128,1024]{2,1,0:T(8,128)(2,1)S(1)}, bf16[1,128,1024]{2,1,0:T(8,128)(2,1)}, u32[]{:S(2)}) copy-start(bf16[1,128,1024]{2,1,0:T(8,128)(2,1)} %param.14) | copy-start | bytes 786436
  241.5 19.1 %copy-start.6 = (f32[128,1024]{1,0:T(8,128)S(1)}, f32[128,1024]{1,0:T(8,128)}, u32[]{:S(2)}) copy-start(f32[128,1024]{1,0:T(8,128)} %copy-done.5) | copy-start | bytes 1572868

commit v2 on v1

--- a/solution.py
+++ b/solution.py
@@ -40,7 +40,8 @@
         pltpu.make_async_copy(src.at[me], dst.at[me], own.at[i]).start()
 
     @pl.loop(1, n)
-    def _(k):
+    def _(step):
+        k = lax.rem(step * (n // 2 - 1), n)
         for i, (src, dst) in enumerate(pairs):
             exchange_copy(n, me, k, src, dst, send.at[i], recv.at[i]).start()
 
@@ -263,7 +264,13 @@
         sends.append(packed(
             jnp.dot(pick, joined, preferred_element_type=bf16).reshape(n, rest * both)
         ))
-    quarters = tokens.reshape(rows, lines, QUAD, -1).transpose(2, 0, 1, 3).reshape(QUAD, rows, -1)
+    depth = width // n
+    quarters = jnp.stack([
+        jnp.concatenate([
+            tokens[:, (j * QUAD + c) * depth:(j * QUAD + c + 1) * depth] for j in range(lines)
+        ], axis=1)
+        for c in range(QUAD)
+    ])
 
     got = forward(n, sends, quarters, base_weight)
     base = got[-1]

time: 273 us -> 256 us (0.938)
  local copies, waits for them, and re-layouts: 23.9 us -> 8.29 us
  Pallas kernels: 222 us -> 226 us
    reshape x3 -> x0, local copies, waits for them, and re-layouts: 12.8 us -> none  [local(): tokens.reshape(rows, lines, QUAD, -1).transpose(2, 0, 1, 3)]
    unnamed x28 -> x22, local copies, waits for them, and re-layouts: 10.2 us -> 5.5 us
    pallas_call x1, Pallas kernels: 13.7 us -> 17.7 us  [back(): pl.pallas_call(functools.partial(back_kernel, n, count), out_shape=[jax.S...]
where the time goes in v2:
time: 256 us; the launch traced here: 255 us
  Pallas kernels  226 us (88%)
  matrix products  16.5 us (6%)
  local copies, waits for them, and re-layouts  8.29 us (3%)
    pallas_call x1, Pallas kernels, forward(): pl.pallas_call(functools.partial(forward_kernel, n, count), out_shape=[ja...  209 us
    pallas_call x1, Pallas kernels, back(): pl.pallas_call(functools.partial(back_kernel, n, count), out_shape=[jax.S...  17.7 us
    dot_general x1, matrix products, local(): lax.dot_general(token_block, low, (((0,), (0,)), ((), ())), preferred_ele...  6.59 us
    unnamed x22, local copies, waits for them, and re-layouts  5.5 us

profile of v2, /device:TPU:1, one launch (start us, length us, event | category | flops | bytes accessed | tf_op | source)
XLA Modules:
  0.0 255.5 jit_solution(12602395893458875669)
XLA Ops:
  0.6 0.0 copy-start
  0.6 1.9 fusion.34
  2.5 0.1 maximum_bitcast_fusion
  2.7 0.1 maximum_bitcast_fusion.2
  2.8 0.0 copy-start.7
  2.8 0.0 copy-start.5
  2.8 0.0 copy-start.3
  2.8 0.3 pad_maximum_fusion.refs_2_
  3.1 0.0 copy-start.4
  3.1 0.3 copy-done.7
  3.5 0.2 convert_reduce_fusion
  3.6 0.0 copy-done.5
  3.6 0.1 select_reduce_fusion
  3.7 0.7 copy-done.3
  4.4 0.1 constant_dynamic-update-slice_fusion.1
  4.6 0.0 copy-done.4
  4.6 1.4 fusion.19
  6.0 0.0 copy-start.2
  6.0 0.4 fusion.27
  6.5 0.7 copy-done.2
  7.2 208.6 %shard_map.103 = (bf16[16,16,9216]{2,1,0:T(8,128)(2,1)S(1)}, bf16[16,16,640]{2,1,0:T(8,128)(2,1)S(1)}, f32[128,1024]{1,0:T(8,128)S(1)}) custom-call(bf16[16,16,9216]{2,1,0:T(8,128)(2,1)S(1)} %bitcast.48, bf16[16,16,640]{2,1,0:T(8,128)(2,1)S(1)} %bitcast.52, bf16[4,128,2048]{2,1,0:T(8,128)(2,1)S(1)} %pad_maximum_fusion.refs_2_, bf16[512,1024]{1,0:T(8,128)(2,1)S(1)} %copy-done.2), custom_call_target="tpu_custom_call" | custom-call | tf_op jit(solution)/shard_map/pallas_call | solution.py:182
  215.9 0.0 copy-start.1
  215.9 0.1 copy.12
  216.0 0.0 copy-start.6
  216.0 2.0 copy-done.1
  218.0 0.0 copy-done.6
  218.0 0.6 fusion.30
  218.6 0.6 iota_compare_fusion.8
  219.3 0.0 copy-done
  219.3 3.5 %fusion.11 = bf16[272,128]{1,0:T(8,128)(2,1)S(1)} fusion(bf16[1,8192,128]{2,1,0:T(8,128)(2,1)S(1)} %copy-done, pred[128]{0:T(512)(128)(4,1)S(1)} %iota_compare_fusion.8, bf16[256,9216]{1,0:T(8,128)(2,1)} %bitcast.50, bf16[16,9216]{1,0:T(8,128)(2,1)S(1)} %slice.88), kind=kOutput, calls=%fused_computation.17 | convolution fusion | flops 579407872 | bytes 7180416 | tf_op jit(solution)/shard_map/dot_general | solution.py:291
  224.1 1.1 fusion.5
  225.3 6.6 %convolution_bitcast_fusion = f32[1,8192,128]{2,1,0:T(8,128)} fusion(bf16[272,1024]{1,0:T(8,128)(2,1)S(1)} %pad_maximum_fusion.1, bf16[1,128,1024]{2,1,0:T(8,128)(2,1)} %param.14, f32[]{:T(128)S(6)} %div.3, pred[128]{0:T(512)(128)(4,1)S(1)} %iota_compare_fusion.8, bf16[256,9216]{1,0:T(8,128)(2,1)} %bitcast.51, bf16[16,9216]{1,0:T(8,128)(2,1)S(1)} %slice.88), kind=kOutput, calls=%fused_computation | convolution fusion | flops 650745856 | bytes 10027140 | tf_op jit(solution)/shard_map/dot_general | solution.py:315
  231.8 1.2 fusion.3
  233.1 0.8 slice.91
  233.9 0.6 copy.13
  234.6 17.7 %shard_map.104 = (bf16[16,16,1024]{2,1,0:T(8,128)(2,1)}, bf16[16,16,128]{2,1,0:T(8,128)(2,1)}) custom-call(bf16[16,16,1024]{2,1,0:T(8,128)(2,1)} %bitcast.54, bf16[16,16,128]{2,1,0:T(8,128)(2,1)} %bitcast.58), custom_call_target="tpu_custom_call" | custom-call | tf_op jit(solution)/shard_map/pallas_call | solution.py:202
  252.3 1.3 fusion.18
  253.6 0.9 copy.16
  254.5 1.0 fusion.6
  (8 shorter events, 0.2 us)
Async XLA Ops:
  0.6 218.6 %copy-start = (bf16[1,8192,128]{2,1,0:T(8,128)(2,1)S(1)}, bf16[1,8192,128]{2,1,0:T(8,128)(2,1)}, u32[]{:S(2)}) copy-start(bf16[1,8192,128]{2,1,0:T(8,128)(2,1)} %param.13) | copy-start | bytes 6291460
  2.8 0.7 copy-start.7
  2.8 0.8 copy-start.5
  2.8 1.6 copy-start.3
  3.1 1.5 copy-start.4
  6.0 1.2 copy-start.2
  215.9 2.1 copy-start.1
  216.0 2.0 copy-start.6

commit v3 on v2

--- a/solution.py
+++ b/solution.py
@@ -18,8 +18,13 @@
     )
 
 
-def greet_all(n, me):
+def greet_all(n, me, shares=1):
     barrier = pltpu.get_barrier_semaphore()
+    if shares == 2:
+        pl.semaphore_signal(
+            barrier, inc=1, device_id={"groups": 1 - lax.axis_index("groups"), "shard": me},
+            device_id_type=MESH,
+        )
 
     @pl.loop(1, n)
     def _(k):
@@ -27,7 +32,7 @@
             barrier, inc=1, device_id={"shard": lax.rem(me + k, n)}, device_id_type=MESH
         )
 
-    pl.semaphore_wait(barrier, n - 1)
+    pl.semaphore_wait(barrier, n - 2 + shares)
 
 
 def exchange_copy(n, me, k, src, dst, send, recv):
@@ -35,11 +40,13 @@
     return remote(src.at[to], dst.at[me], send.at[k], recv.at[k], to)
 
 
-def start_exchange(n, me, pairs, send, recv, own):
+def start_own(me, pairs, own):
     for i, (src, dst) in enumerate(pairs):
         pltpu.make_async_copy(src.at[me], dst.at[me], own.at[i]).start()
 
-    @pl.loop(1, n)
+
+def start_exchange(n, me, pairs, send, recv, first, last):
+    @pl.loop(first, last)
     def _(step):
         k = lax.rem(step * (n // 2 - 1), n)
         for i, (src, dst) in enumerate(pairs):
@@ -61,24 +68,35 @@
     send, recv, own = refs[2 * count:]
     me = lax.axis_index("shard")
     greet_all(n, me)
-    start_exchange(n, me, pairs, send, recv, own)
+    start_own(me, pairs, own)
+    start_exchange(n, me, pairs, send, recv, 1, n)
     finish_exchange(n, me, pairs, send, recv, own)
 
 
-def forward_kernel(n, count, *refs):
+def forward_kernel(n, count, shares, *refs):
     ins, outs = refs[:count], refs[count + 2:2 * count + 2]
     quarters_ref, weight_ref = refs[count:count + 2]
     base_ref = refs[2 * count + 2]
     (quad_tokens, weights, partial, partial_in, send, recv, own,
-     w_right, w_left, w_recv, t_send, t_recv, p_send, p_recv, local_sem) = refs[2 * count + 3:]
+     w_right, w_left, w_recv, y_send, y_recv, t_send, t_recv, p_send, p_recv, local_sem) = refs[2 * count + 3:]
     pairs = list(zip(ins, outs))
     me = lax.axis_index("shard")
     lines = n // QUAD
     row, col = me // QUAD, lax.rem(me, QUAD)
     depth = weight_ref.shape[0]
 
+    group = lax.axis_index("groups")
+    half = depth // shares
+
     def block(j):
-        return weights.at[pl.ds(pl.multiple_of(j * depth, depth), depth)]
+        first = j * depth + (group * half if shares == 2 else 0)
+        return weights.at[pl.ds(pl.multiple_of(first, half), half)]
+
+    def across(j):
+        return pltpu.make_async_remote_copy(
+            src_ref=block(j), dst_ref=block(j), send_sem=y_send.at[j], recv_sem=y_recv.at[j],
+            device_id={"groups": 1 - group, "shard": me}, device_id_type=MESH,
+        )
 
     def to_right(j):
         return remote(block(j), block(j), w_right.at[j], w_recv.at[j], me + QUAD)
@@ -96,11 +114,13 @@
         return remote(partial.at[other], partial_in.at[col], p_send.at[k], p_recv.at[k],
                       row * QUAD + other)
 
-    own_weight = pltpu.make_async_copy(weight_ref, block(row), local_sem.at[0])
+    own_weight = pltpu.make_async_copy(
+        weight_ref, weights.at[pl.ds(pl.multiple_of(row * depth, depth), depth)], local_sem.at[0]
+    )
     own_tokens = pltpu.make_async_copy(quarters_ref.at[col], quad_tokens.at[col], local_sem.at[1])
     own_weight.start()
     own_tokens.start()
-    greet_all(n, me)
+    greet_all(n, me, shares)
     own_weight.wait()
 
     @pl.when(row < lines - 1)
@@ -113,10 +133,14 @@
 
     for k in range(1, QUAD):
         token_copy(k).start()
-    start_exchange(n, me, pairs, send, recv, own)
+    start_own(me, pairs, own)
+    step = -(-(n - 1) // (lines - 1))
 
     @pl.loop(1, lines)
     def _(t):
+        start_exchange(n, me, pairs, send, recv, 1 + (t - 1) * step,
+                       jnp.minimum(1 + t * step, n))
+
         @pl.when(row - t >= 0)
         def _():
             to_right(row - t).wait_recv()
@@ -125,6 +149,9 @@
             def _():
                 to_right(row - t).start()
 
+            if shares == 2:
+                across(row - t).start()
+
         @pl.when(row + t <= lines - 1)
         def _():
             to_left(row + t).wait_recv()
@@ -132,6 +159,16 @@
             @pl.when(row > 0)
             def _():
                 to_left(row + t).start()
+
+            if shares == 2:
+                across(row + t).start()
+
+    if shares == 2:
+        @pl.loop(0, lines)
+        def _(j):
+            @pl.when(j != row)
+            def _():
+                across(j).wait()
 
     own_tokens.wait()
     for k in range(1, QUAD):
@@ -176,11 +213,12 @@
 def forward(n, sends, quarters, base_weight):
     count = len(sends)
     lines = n // QUAD
+    shares = 2 if lax.axis_size("groups") == 2 and base_weight.shape[0] % 32 == 0 else 1
     rows, quarter = quarters.shape[1:]
     wide = base_weight.shape[1]
     dma = pltpu.SemaphoreType.DMA
     return pl.pallas_call(
-        functools.partial(forward_kernel, n, count),
+        functools.partial(forward_kernel, n, count, shares),
         out_shape=[jax.ShapeDtypeStruct(s.shape, s.dtype) for s in sends]
         + [jax.ShapeDtypeStruct((rows, wide), jnp.float32)],
         in_specs=[ANY] * (count + 2),
@@ -190,7 +228,7 @@
             pltpu.VMEM((quarter, wide), jnp.bfloat16),
             pltpu.VMEM((QUAD, rows, wide), jnp.float32),
             pltpu.VMEM((QUAD, rows, wide), jnp.float32),
-        ] + exchange_sems(n, count) + [dma((lines,))] * 3 + [dma((QUAD,))] * 4 + [dma((2,))],
+        ] + exchange_sems(n, count) + [dma((lines,))] * 5 + [dma((QUAD,))] * 4 + [dma((2,))],
         compiler_params=pltpu.CompilerParams(
             collective_id=0, has_side_effects=True, vmem_limit_bytes=40 * 2**20
         ),

time: 256 us -> 216 us (0.84)
  Pallas kernels: 226 us -> 187 us
    pallas_call x1, Pallas kernels: 209 us -> 149 us  [forward(): pl.pallas_call(functools.partial(forward_kernel, n, count, shares), out_s...]
    pallas_call x1, Pallas kernels: 17.7 us -> 37.2 us  [back(): pl.pallas_call(functools.partial(back_kernel, n, count), out_shape=[jax.S...]
where the time goes in v3:
time: 216 us
  Pallas kernels  187 us (87%)
  matrix products  16.5 us (8%)
  local copies, waits for them, and re-layouts  8.29 us (4%)
  between operations  2.21 us (1%)
    pallas_call x1, Pallas kernels, forward(): pl.pallas_call(functools.partial(forward_kernel, n, count, shares), out_s...  149 us
    pallas_call x1, Pallas kernels, back(): pl.pallas_call(functools.partial(back_kernel, n, count), out_shape=[jax.S...  37.2 us
    dot_general x1, matrix products, local(): lax.dot_general(token_block, low, (((0,), (0,)), ((), ())), preferred_ele...  6.59 us
    unnamed x22, local copies, waits for them, and re-layouts  5.5 us

profile of v3, /device:TPU:1, one launch (start us, length us, event | category | flops | bytes accessed | tf_op | source)
XLA Modules:
  0.0 215.7 jit_solution(12724617458536322160)
XLA Ops:
  0.6 0.0 copy-start
  0.6 1.9 fusion.34
  2.5 0.1 maximum_bitcast_fusion
  2.7 0.1 maximum_bitcast_fusion.2
  2.8 0.0 copy-start.7
  2.8 0.0 copy-start.5
  2.8 0.0 copy-start.3
  2.8 0.3 pad_maximum_fusion.refs_2_
  3.1 0.0 copy-start.4
  3.1 0.3 copy-done.7
  3.5 0.2 convert_reduce_fusion
  3.6 0.0 copy-done.5
  3.6 0.1 select_reduce_fusion
  3.7 0.7 copy-done.3
  4.4 0.1 constant_dynamic-update-slice_fusion.1
  4.6 0.0 copy-done.4
  4.6 1.4 fusion.19
  6.0 0.0 copy-start.2
  6.0 0.4 fusion.27
  6.5 0.7 copy-done.2
  7.2 149.4 %shard_map.103 = (bf16[16,16,9216]{2,1,0:T(8,128)(2,1)S(1)}, bf16[16,16,640]{2,1,0:T(8,128)(2,1)S(1)}, f32[128,1024]{1,0:T(8,128)S(1)}) custom-call(bf16[16,16,9216]{2,1,0:T(8,128)(2,1)S(1)} %bitcast.48, bf16[16,16,640]{2,1,0:T(8,128)(2,1)S(1)} %bitcast.52, bf16[4,128,2048]{2,1,0:T(8,128)(2,1)S(1)} %pad_maximum_fusion.refs_2_, bf16[512,1024]{1,0:T(8,128)(2,1)S(1)} %copy-done.2), custom_call_target="tpu_custom_call" | custom-call | tf_op jit(solution)/shard_map/pallas_call | solution.py:220
  156.6 0.0 copy-start.1
  156.7 0.1 copy.12
  156.8 0.0 copy-start.6
  156.8 2.0 copy-done.1
  158.8 0.0 copy-done.6
  158.8 0.6 fusion.30
  159.4 0.6 iota_compare_fusion.8
  160.1 0.0 copy-done
  160.1 3.5 %fusion.11 = bf16[272,128]{1,0:T(8,128)(2,1)S(1)} fusion(bf16[1,8192,128]{2,1,0:T(8,128)(2,1)S(1)} %copy-done, pred[128]{0:T(512)(128)(4,1)S(1)} %iota_compare_fusion.8, bf16[256,9216]{1,0:T(8,128)(2,1)} %bitcast.50, bf16[16,9216]{1,0:T(8,128)(2,1)S(1)} %slice.88), kind=kOutput, calls=%fused_computation.17 | convolution fusion | flops 579407872 | bytes 7180416 | tf_op jit(solution)/shard_map/dot_general | solution.py:329
  164.9 1.1 fusion.5
  166.0 6.6 %convolution_bitcast_fusion = f32[1,8192,128]{2,1,0:T(8,128)} fusion(bf16[272,1024]{1,0:T(8,128)(2,1)S(1)} %pad_maximum_fusion.1, bf16[1,128,1024]{2,1,0:T(8,128)(2,1)} %param.14, f32[]{:T(128)S(6)} %div.3, pred[128]{0:T(512)(128)(4,1)S(1)} %iota_compare_fusion.8, bf16[256,9216]{1,0:T(8,128)(2,1)} %bitcast.51, bf16[16,9216]{1,0:T(8,128)(2,1)S(1)} %slice.88), kind=kOutput, calls=%fused_computation | convolution fusion | flops 650745856 | bytes 10027140 | tf_op jit(solution)/shard_map/dot_general | solution.py:353
  172.6 1.2 fusion.3
  173.9 0.8 slice.91
  174.7 0.6 copy.13
  175.4 37.2 %shard_map.104 = (bf16[16,16,1024]{2,1,0:T(8,128)(2,1)}, bf16[16,16,128]{2,1,0:T(8,128)(2,1)}) custom-call(bf16[16,16,1024]{2,1,0:T(8,128)(2,1)} %bitcast.54, bf16[16,16,128]{2,1,0:T(8,128)(2,1)} %bitcast.58), custom_call_target="tpu_custom_call" | custom-call | tf_op jit(solution)/shard_map/pallas_call | solution.py:240
  212.6 1.3 fusion.18
  213.9 0.9 copy.16
  214.8 1.0 fusion.6
  (8 shorter events, 0.2 us)
Async XLA Ops:
  0.6 159.4 %copy-start = (bf16[1,8192,128]{2,1,0:T(8,128)(2,1)S(1)}, bf16[1,8192,128]{2,1,0:T(8,128)(2,1)}, u32[]{:S(2)}) copy-start(bf16[1,8192,128]{2,1,0:T(8,128)(2,1)} %param.13) | copy-start | bytes 6291460
  2.8 0.7 copy-start.7
  2.8 0.8 copy-start.5
  2.8 1.6 copy-start.3
  3.1 1.5 copy-start.4
  6.0 1.2 copy-start.2
  156.6 2.1 copy-start.1
  156.8 2.0 copy-start.6
